TPU v7x, 32 devices: a whole 2x2x4 slice. The times are simulated.
32 devices in a mesh: dp: 2 (over core), expert: 16 (over z, y, x).
Axes of the slice: x: 2, y: 2, z: 4, core: 2. Of those that a mesh axis runs over, the one named last changes fastest.
Arguments:
- tokens: bfloat16 [8192, 3584], P(('dp', 'expert')), may hold values from -6 to 6
- cotangent: bfloat16 [8192, 3584], P(('dp', 'expert')), may hold values from -6 to 6
- expert_ids: int32 [8192, 1], P(('dp', 'expert')), may hold values from 0 to 15; in each aligned block of 256 rows (0 to 255, 256 to 511, ...) at most 32 rows name the same one
- gate_probs: float32 [8192, 1], P(('dp', 'expert')), may hold values from 0.2 to 1
- w_gate: bfloat16 [16, 3584, 1024], P('expert', None, 'dp'), may hold values from -0.09375 to 0.09375
- w_up: bfloat16 [16, 3584, 1024], P('expert', None, 'dp'), may hold values from -0.09375 to 0.09375
- w_down: bfloat16 [16, 1024, 3584], P('expert', 'dp'), may hold values from -0.1875 to 0.1875
Outputs:
- grad_tokens: bfloat16 [8192, 3584], P(('dp', 'expert'))
- grad_gate: bfloat16 [16, 3584, 1024], P('expert', None, 'dp')
- grad_up: bfloat16 [16, 3584, 1024], P('expert', None, 'dp')
- grad_down: bfloat16 [16, 1024, 3584], P('expert', 'dp')
Inputs may be any that keep to these rules, and one draw needn't show every extreme that they name: `expert_ids`: within the entries of one device's 256 tokens, no expert is named more than 32 times, and in some device one expert is named exactly 32 times. Each row names exactly one expert.
All inputs are finite; a program needn't handle non-finite values.
Results may differ from a plain program's by a relative error of at most 0.0065.
Values may be sent and summed in bfloat16 or wider, within the bound.
A program may use at most 192 MiB of HBM per device.

v0:
```python
import jax
import jax.numpy as jnp
from jax import lax
from jax.sharding import PartitionSpec as P


def front_rows(rows_x, rows_cot, gate_w, up_w, down_w):
    gate_pre = jnp.dot(rows_x, gate_w, preferred_element_type=jnp.float32)
    up_pre = jnp.dot(rows_x, up_w, preferred_element_type=jnp.float32)
    sigmoid_gate = jax.nn.sigmoid(gate_pre)
    swish_gate = gate_pre * sigmoid_gate
    hidden = (swish_gate * up_pre).astype(jnp.bfloat16)
    d_hidden = lax.dot_general(
        rows_cot, down_w, (((1,), (1,)), ((), ())), preferred_element_type=jnp.float32
    )
    d_gate = (d_hidden * up_pre * sigmoid_gate * (1.0 + gate_pre * (1.0 - sigmoid_gate))).astype(
        jnp.bfloat16
    )
    d_up = (d_hidden * swish_gate).astype(jnp.bfloat16)
    dx_part = lax.dot_general(
        d_gate, gate_w, (((1,), (1,)), ((), ())), preferred_element_type=jnp.float32
    )
    dx_part = dx_part + lax.dot_general(
        d_up, up_w, (((1,), (1,)), ((), ())), preferred_element_type=jnp.float32
    )
    return (hidden, d_gate, d_up, dx_part.astype(jnp.bfloat16))


def weight_sums(rows_x, rows_cot, hidden, d_gate, d_up):
    grad_gate = lax.dot_general(
        rows_x, d_gate, (((0,), (0,)), ((), ())), preferred_element_type=jnp.float32
    )
    grad_up = lax.dot_general(
        rows_x, d_up, (((0,), (0,)), ((), ())), preferred_element_type=jnp.float32
    )
    grad_down = lax.dot_general(
        hidden, rows_cot, (((0,), (0,)), ((), ())), preferred_element_type=jnp.float32
    )
    return (grad_gate, grad_up, grad_down)


def live_of(counts_three, capacity):
    return (jnp.arange(capacity, dtype=jnp.int32) < counts_three).reshape(-1)


def tile_flags(counts_three, capacity):
    live_rows = live_of(counts_three, capacity).astype(jnp.int32)
    return jnp.max(live_rows.reshape(-1, 128), axis=1) > 0


def run_front(rows_four, cots_four, counts_three, weights, capacity):
    model_width = rows_four.shape[-1]
    rows_flat = rows_four.reshape(-1, model_width)
    cots_flat = cots_four.reshape(-1, model_width)
    slot_count = rows_flat.shape[0]
    hidden_width = weights[0].shape[1]
    spare_rows = -slot_count % 128
    tiles_all = (slot_count + spare_rows) // 128
    flags = tile_flags(counts_three, capacity)

    def empty_tile():
        return (
            jnp.zeros((128, hidden_width), jnp.bfloat16),
            jnp.zeros((128, hidden_width), jnp.bfloat16),
            jnp.zeros((128, hidden_width), jnp.bfloat16),
            jnp.zeros((128, model_width), jnp.bfloat16),
        )

    def add_tile(index_tile, outputs):
        start = index_tile * 128
        tile_x = lax.dynamic_slice_in_dim(rows_flat, start, 128)
        tile_cot = lax.dynamic_slice_in_dim(cots_flat, start, 128)
        tile_out = lax.cond(
            flags[index_tile],
            lambda: front_rows(tile_x, tile_cot, weights[0], weights[1], weights[2]),
            empty_tile,
        )
        return tuple(
            (
                lax.dynamic_update_slice_in_dim(whole, piece, start, 0)
                for whole, piece in zip(outputs, tile_out)
            )
        )

    total_rows = slot_count + spare_rows
    initial = (
        jnp.zeros((total_rows, hidden_width), jnp.bfloat16),
        jnp.zeros((total_rows, hidden_width), jnp.bfloat16),
        jnp.zeros((total_rows, hidden_width), jnp.bfloat16),
        jnp.zeros((total_rows, model_width), jnp.bfloat16),
    )
    outputs = lax.fori_loop(0, tiles_all, add_tile, initial)
    results = tuple((whole for whole in outputs))
    return results


def run_sums(rows_x, rows_cot, hidden, d_gate, d_up, counts_three, capacity):
    slot_count = rows_x.shape[0]
    model_width = rows_x.shape[1]
    hidden_width = hidden.shape[1]
    spare_rows = -slot_count % 128
    tiles_all = (slot_count + spare_rows) // 128
    sources = [source for source in (rows_x, rows_cot, hidden, d_gate, d_up)]
    flags = tile_flags(counts_three, capacity)

    def add_tile(index_tile, totals):
        start = index_tile * 128
        operands = [lax.dynamic_slice_in_dim(source, start, 128) for source in sources]

        def with_tile():
            added = weight_sums(operands[0], operands[1], operands[2], operands[3], operands[4])
            return tuple((running + extra for running, extra in zip(totals, added)))

        return lax.cond(flags[index_tile], with_tile, lambda: totals)

    initial = (
        jnp.zeros((model_width, hidden_width), jnp.float32),
        jnp.zeros((model_width, hidden_width), jnp.float32),
        jnp.zeros((hidden_width, model_width), jnp.float32),
    )
    sums = lax.fori_loop(0, tiles_all, add_tile, initial)
    return sums


def local(tokens, cotangent, expert_ids, gate_probs, w_gate, w_up, w_down):
    owners = lax.axis_size("expert")
    groups = lax.axis_size("dp")
    tok_rows = tokens.shape[0]
    model_width = tokens.shape[1]
    fanout = expert_ids.shape[1]
    capacity = max(2, 2 * tok_rows * fanout // owners)
    copies = tok_rows * fanout
    flat_ids = expert_ids.reshape(copies)
    onehot = (flat_ids[:, None] == jnp.arange(owners, dtype=jnp.int32)[None, :]).astype(jnp.int32)
    before = jnp.cumsum(onehot, axis=0) - onehot
    slot_rank = jnp.sum(before * onehot, axis=1)
    counts = jnp.sum(onehot, axis=0).reshape(owners, 1)
    position = flat_ids * capacity + slot_rank
    copy_rows = tokens[:, None, :].reshape(copies, model_width)
    copy_tok_cot = cotangent[:, None, :].reshape(copies, model_width)
    copy_cots = (gate_probs * copy_tok_cot.astype(jnp.float32)).astype(jnp.bfloat16)
    placing = (jnp.arange(owners * capacity, dtype=jnp.int32)[:, None] == position[None, :]).astype(
        jnp.bfloat16
    )
    sent_rows = (
        jnp.dot(placing, copy_rows, preferred_element_type=jnp.float32)
        .astype(jnp.bfloat16)
        .reshape(owners, capacity, model_width)
    )
    sent_cots = (
        jnp.dot(placing, copy_cots, preferred_element_type=jnp.float32)
        .astype(jnp.bfloat16)
        .reshape(owners, capacity, model_width)
    )
    came_rows, came_cots, came_counts = (
        lax.all_to_all(sent_rows, "expert", split_axis=0, concat_axis=0, tiled=True),
        lax.all_to_all(sent_cots, "expert", split_axis=0, concat_axis=0, tiled=True),
        lax.all_to_all(counts, "expert", split_axis=0, concat_axis=0, tiled=True),
    )
    got_rows, got_cots, got_counts = (
        lax.all_gather(came_rows, "dp", axis=0, tiled=True),
        lax.all_gather(came_cots, "dp", axis=0, tiled=True),
        lax.all_gather(came_counts, "dp", axis=0, tiled=True),
    )
    got_rows = got_rows.reshape(groups, owners, capacity, model_width)
    got_cots = got_cots.reshape(groups, owners, capacity, model_width)
    got_counts = got_counts.reshape(groups, owners, 1)
    slots_all = owners * groups * capacity
    weights_own = (w_gate[0], w_up[0], w_down[0])
    hidden, d_gate, d_up, dx_part = run_front(got_rows, got_cots, got_counts, weights_own, capacity)
    rows_x = got_rows.reshape(slots_all, model_width)
    rows_cot = got_cots.reshape(slots_all, model_width)
    grad_gate, grad_up, grad_down = run_sums(
        rows_x, rows_cot, hidden, d_gate, d_up, got_counts, capacity
    )
    dx_float = dx_part.astype(jnp.float32)
    summed = lax.psum_scatter(
        dx_float.reshape(groups * owners, capacity, model_width).astype(jnp.bfloat16),
        "dp",
        scatter_dimension=0,
        tiled=True,
    )
    returned = lax.all_to_all(summed, "expert", split_axis=0, concat_axis=0, tiled=True)
    copy_grad = lax.dot_general(
        placing,
        returned.reshape(owners * capacity, model_width),
        (((0,), (0,)), ((), ())),
        preferred_element_type=jnp.float32,
    )
    grad_tokens = jnp.sum(copy_grad.reshape(tok_rows, fanout, model_width), axis=1).astype(
        jnp.bfloat16
    )
    return (
        grad_tokens,
        grad_gate.astype(jnp.bfloat16)[None],
        grad_up.astype(jnp.bfloat16)[None],
        grad_down.astype(jnp.bfloat16)[None],
    )


def solution(mesh):
    return jax.shard_map(
        local,
        mesh=mesh,
        in_specs=(
            P(("dp", "expert"), None),
            P(("dp", "expert"), None),
            P(("dp", "expert"), None),
            P(("dp", "expert"), None),
            P("expert", None, "dp"),
            P("expert", None, "dp"),
            P("expert", "dp", None),
        ),
        out_specs=(
            P(("dp", "expert"), None),
            P("expert", None, "dp"),
            P("expert", None, "dp"),
            P("expert", "dp", None),
        ),
        check_vma=False,
    )
```

profile of v0, /device:TPU:14, one launch (start us, length us, event | category | flops | bytes accessed | tf_op | source)
XLA Modules:
  0.0 592.3 jit_solution(8586603339494069426)
XLA Ops:
  13.1 87.5 %all_to_all.27 = bf16[16,32,3584]{2,1,0:T(8,128)(2,1)} all-to-all(bf16[16,32,3584]{2,1,0:T(8,128)(2,1)S(1)} %bitcast.50), channel_id=1, replica_groups=mesh['dp'=2,'expert'=16] {'expert'}, dimensions={0} | all-to-all | bytes 7340032 | tf_op jit(solution)/shard_map/all_to_all | solution.py:157
  101.8 85.8 %all_to_all.28 = bf16[16,32,3584]{2,1,0:T(8,128)(2,1)} all-to-all(bf16[16,32,3584]{2,1,0:T(8,128)(2,1)S(1)} %bitcast.51), channel_id=1, replica_groups=mesh['dp'=2,'expert'=16] {'expert'}, dimensions={0} | all-to-all | bytes 7340032 | tf_op jit(solution)/shard_map/all_to_all | solution.py:156
  212.9 142.5 %while.36 = (s32[]{:T(128)}, bf16[1024,512]{1,0:T(8,128)(2,1)}, bf16[1024,512]{1,0:T(8,128)(2,1)}, bf16[1024,512]{1,0:T(8,128)(2,1)}, bf16[1024,3584]{1,0:T(8,12...) while((s32[]{:T(128)}, bf16[1024,512]{1,0:T(8,128)(2,1)}, ...), condition=%wide.region_9.10_spmd, body=%wide.region_6.9_spmd.sunk | while | flops 2350710784 | bytes 74059120 | solution.py:92
  214.1 13.2 %conditional.4 = (bf16[128,512]{1,0:T(8,128)(2,1)S(1)}, bf16[128,512]{1,0:T(8,128)(2,1)}, bf16[128,512]{1,0:T(8,128)(2,1)}, bf16[128,3584]{1,0:T(8,128)(2,1)S(1)}) conditional(s32[]{:T(128)} %bitcast.44, () %tuple.97, (bf16[1024,3584]{1,0:T(8,128)(2,1)}, s32[]{:T(128)}, bf16[3584,512]{1,0:T(8,128)(2,1)}, bf16[3584,512]{1,0:T(8,128)(2,1)}, ...), branch_computations={%region_7.7_spmd, %region_8.8_spmd} | conditional | flops 2350710784 | bytes 71435888 | solution.py:73
  232.0 13.2 %conditional.4 = (bf16[128,512]{1,0:T(8,128)(2,1)S(1)}, bf16[128,512]{1,0:T(8,128)(2,1)}, bf16[128,512]{1,0:T(8,128)(2,1)}, bf16[128,3584]{1,0:T(8,128)(2,1)S(1)}) conditional(s32[]{:T(128)} %bitcast.44, () %tuple.97, (bf16[1024,3584]{1,0:T(8,128)(2,1)}, s32[]{:T(128)}, bf16[3584,512]{1,0:T(8,128)(2,1)}, bf16[3584,512]{1,0:T(8,128)(2,1)}, ...), branch_computations={%region_7.7_spmd, %region_8.8_spmd} | conditional | flops 2350710784 | bytes 71435888 | solution.py:73
  249.8 13.2 %conditional.4 = (bf16[128,512]{1,0:T(8,128)(2,1)S(1)}, bf16[128,512]{1,0:T(8,128)(2,1)}, bf16[128,512]{1,0:T(8,128)(2,1)}, bf16[128,3584]{1,0:T(8,128)(2,1)S(1)}) conditional(s32[]{:T(128)} %bitcast.44, () %tuple.97, (bf16[1024,3584]{1,0:T(8,128)(2,1)}, s32[]{:T(128)}, bf16[3584,512]{1,0:T(8,128)(2,1)}, bf16[3584,512]{1,0:T(8,128)(2,1)}, ...), branch_computations={%region_7.7_spmd, %region_8.8_spmd} | conditional | flops 2350710784 | bytes 71435888 | solution.py:73
  267.6 13.2 %conditional.4 = (bf16[128,512]{1,0:T(8,128)(2,1)S(1)}, bf16[128,512]{1,0:T(8,128)(2,1)}, bf16[128,512]{1,0:T(8,128)(2,1)}, bf16[128,3584]{1,0:T(8,128)(2,1)S(1)}) conditional(s32[]{:T(128)} %bitcast.44, () %tuple.97, (bf16[1024,3584]{1,0:T(8,128)(2,1)}, s32[]{:T(128)}, bf16[3584,512]{1,0:T(8,128)(2,1)}, bf16[3584,512]{1,0:T(8,128)(2,1)}, ...), branch_computations={%region_7.7_spmd, %region_8.8_spmd} | conditional | flops 2350710784 | bytes 71435888 | solution.py:73
  285.4 13.2 %conditional.4 = (bf16[128,512]{1,0:T(8,128)(2,1)S(1)}, bf16[128,512]{1,0:T(8,128)(2,1)}, bf16[128,512]{1,0:T(8,128)(2,1)}, bf16[128,3584]{1,0:T(8,128)(2,1)S(1)}) conditional(s32[]{:T(128)} %bitcast.44, () %tuple.97, (bf16[1024,3584]{1,0:T(8,128)(2,1)}, s32[]{:T(128)}, bf16[3584,512]{1,0:T(8,128)(2,1)}, bf16[3584,512]{1,0:T(8,128)(2,1)}, ...), branch_computations={%region_7.7_spmd, %region_8.8_spmd} | conditional | flops 2350710784 | bytes 71435888 | solution.py:73
  303.2 13.2 %conditional.4 = (bf16[128,512]{1,0:T(8,128)(2,1)S(1)}, bf16[128,512]{1,0:T(8,128)(2,1)}, bf16[128,512]{1,0:T(8,128)(2,1)}, bf16[128,3584]{1,0:T(8,128)(2,1)S(1)}) conditional(s32[]{:T(128)} %bitcast.44, () %tuple.97, (bf16[1024,3584]{1,0:T(8,128)(2,1)}, s32[]{:T(128)}, bf16[3584,512]{1,0:T(8,128)(2,1)}, bf16[3584,512]{1,0:T(8,128)(2,1)}, ...), branch_computations={%region_7.7_spmd, %region_8.8_spmd} | conditional | flops 2350710784 | bytes 71435888 | solution.py:73
  321.1 13.2 %conditional.4 = (bf16[128,512]{1,0:T(8,128)(2,1)S(1)}, bf16[128,512]{1,0:T(8,128)(2,1)}, bf16[128,512]{1,0:T(8,128)(2,1)}, bf16[128,3584]{1,0:T(8,128)(2,1)S(1)}) conditional(s32[]{:T(128)} %bitcast.44, () %tuple.97, (bf16[1024,3584]{1,0:T(8,128)(2,1)}, s32[]{:T(128)}, bf16[3584,512]{1,0:T(8,128)(2,1)}, bf16[3584,512]{1,0:T(8,128)(2,1)}, ...), branch_computations={%region_7.7_spmd, %region_8.8_spmd} | conditional | flops 2350710784 | bytes 71435888 | solution.py:73
  338.9 13.2 %conditional.4 = (bf16[128,512]{1,0:T(8,128)(2,1)S(1)}, bf16[128,512]{1,0:T(8,128)(2,1)}, bf16[128,512]{1,0:T(8,128)(2,1)}, bf16[128,3584]{1,0:T(8,128)(2,1)S(1)}) conditional(s32[]{:T(128)} %bitcast.44, () %tuple.97, (bf16[1024,3584]{1,0:T(8,128)(2,1)}, s32[]{:T(128)}, bf16[3584,512]{1,0:T(8,128)(2,1)}, bf16[3584,512]{1,0:T(8,128)(2,1)}, ...), branch_computations={%region_7.7_spmd, %region_8.8_spmd} | conditional | flops 2350710784 | bytes 71435888 | solution.py:73
  355.5 17.2 %reduce-scatter.2.cloned.1.call-done = bf16[16,32,3584]{2,1,0:T(8,128)(2,1)} async-done(((bf16[32,32,3584]{2,1,0:T(8,128)(2,1)}), bf16[16,32,3584]{2,1,0:T(8,128)(2,1)}) %reduce-scatter.2.cloned.1.call-update) | async-done | bytes 3670032 | tf_op jit(solution)/shard_map/reduce_scatter | solution.py:177
  391.3 175.4 %while.37 = (s32[]{:T(128)}, f32[3584,512]{1,0:T(8,128)}, f32[3584,512]{1,0:T(8,128)}, f32[512,3584]{1,0:T(8,128)}, pred[8]{0:T(512)(128)(4,1)S(1)}, /*index=5*/...) while((s32[]{:T(128)}, f32[3584,512]{1,0:T(8,128)}, ...), condition=%wide.region_14.15_spmd, body=%wide.region_11.14_spmd.sunk | while | flops 1414791168 | bytes 105909608 | solution.py:121
  392.5 20.7 %conditional.5 = ((f32[3584,512]{1,0:T(8,128)}, f32[3584,512]{1,0:T(8,128)}, f32[512,3584]{1,0:T(8,128)})) conditional(s32[]{:T(128)} %bitcast.45, (f32[3584,512]{1,0:T(8,128)}, f32[3584,512]{1,0:T(8,128)}, f32[512,3584]{1,0:T(8,128)}) %tuple.100, (s32[]{:T(128)}, bf16[1024,3584]{1,0:T(8,128)(2,1)}, bf16[1024,512]{1,0:T(8,128)(2,1)}, ...), branch_computations={%region_12.12_spmd, %region_13.13_spmd} | conditional | flops 1414791168 | bytes 105909384 | solution.py:114
  403.0 10.2 %convolution_add_fusion.2 = f32[3584,512]{1,0:T(8,128)} fusion(f32[3584,512]{1,0:T(8,128)} %get-tuple-element.538, bf16[1024,3584]{1,0:T(8,128)(2,1)} %get-tuple-element.535, s32[]{:T(128)S(6)} %select_n.35, bf16[1024,512]{1,0:T(8,128)(2,1)} %get-tuple-element.539), kind=kOutput, calls=%fused_computation.21 | convolution fusion | flops 471597056 | bytes 15729664 | tf_op jit(solution)/shard_map/while/body/eval_jaxpr/cond/branch_1_fun/dot_general | solution.py:33
  414.5 20.7 %conditional.5 = ((f32[3584,512]{1,0:T(8,128)}, f32[3584,512]{1,0:T(8,128)}, f32[512,3584]{1,0:T(8,128)})) conditional(s32[]{:T(128)} %bitcast.45, (f32[3584,512]{1,0:T(8,128)}, f32[3584,512]{1,0:T(8,128)}, f32[512,3584]{1,0:T(8,128)}) %tuple.100, (s32[]{:T(128)}, bf16[1024,3584]{1,0:T(8,128)(2,1)}, bf16[1024,512]{1,0:T(8,128)(2,1)}, ...), branch_computations={%region_12.12_spmd, %region_13.13_spmd} | conditional | flops 1414791168 | bytes 105909384 | solution.py:114
  414.5 7.6 %convolution_add_fusion.3 = f32[3584,512]{1,0:T(8,128)} fusion(f32[3584,512]{1,0:T(8,128)} %get-tuple-element.534, bf16[1024,3584]{1,0:T(8,128)(2,1)} %get-tuple-element.535, s32[]{:T(128)S(6)} %select_n.35, bf16[1024,512]{1,0:T(8,128)(2,1)} %get-tuple-element.537), kind=kOutput, calls=%fused_computation.22 | convolution fusion | flops 471597056 | bytes 15729664 | tf_op jit(solution)/shard_map/while/body/eval_jaxpr/cond/branch_1_fun/dot_general | solution.py:30
  424.9 10.2 %convolution_add_fusion.2 = f32[3584,512]{1,0:T(8,128)} fusion(f32[3584,512]{1,0:T(8,128)} %get-tuple-element.538, bf16[1024,3584]{1,0:T(8,128)(2,1)} %get-tuple-element.535, s32[]{:T(128)S(6)} %select_n.35, bf16[1024,512]{1,0:T(8,128)(2,1)} %get-tuple-element.539), kind=kOutput, calls=%fused_computation.21 | convolution fusion | flops 471597056 | bytes 15729664 | tf_op jit(solution)/shard_map/while/body/eval_jaxpr/cond/branch_1_fun/dot_general | solution.py:33
  436.4 20.7 %conditional.5 = ((f32[3584,512]{1,0:T(8,128)}, f32[3584,512]{1,0:T(8,128)}, f32[512,3584]{1,0:T(8,128)})) conditional(s32[]{:T(128)} %bitcast.45, (f32[3584,512]{1,0:T(8,128)}, f32[3584,512]{1,0:T(8,128)}, f32[512,3584]{1,0:T(8,128)}) %tuple.100, (s32[]{:T(128)}, bf16[1024,3584]{1,0:T(8,128)(2,1)}, bf16[1024,512]{1,0:T(8,128)(2,1)}, ...), branch_computations={%region_12.12_spmd, %region_13.13_spmd} | conditional | flops 1414791168 | bytes 105909384 | solution.py:114
  436.4 7.6 %convolution_add_fusion.3 = f32[3584,512]{1,0:T(8,128)} fusion(f32[3584,512]{1,0:T(8,128)} %get-tuple-element.534, bf16[1024,3584]{1,0:T(8,128)(2,1)} %get-tuple-element.535, s32[]{:T(128)S(6)} %select_n.35, bf16[1024,512]{1,0:T(8,128)(2,1)} %get-tuple-element.537), kind=kOutput, calls=%fused_computation.22 | convolution fusion | flops 471597056 | bytes 15729664 | tf_op jit(solution)/shard_map/while/body/eval_jaxpr/cond/branch_1_fun/dot_general | solution.py:30
  446.8 10.2 %convolution_add_fusion.2 = f32[3584,512]{1,0:T(8,128)} fusion(f32[3584,512]{1,0:T(8,128)} %get-tuple-element.538, bf16[1024,3584]{1,0:T(8,128)(2,1)} %get-tuple-element.535, s32[]{:T(128)S(6)} %select_n.35, bf16[1024,512]{1,0:T(8,128)(2,1)} %get-tuple-element.539), kind=kOutput, calls=%fused_computation.21 | convolution fusion | flops 471597056 | bytes 15729664 | tf_op jit(solution)/shard_map/while/body/eval_jaxpr/cond/branch_1_fun/dot_general | solution.py:33
  458.3 20.7 %conditional.5 = ((f32[3584,512]{1,0:T(8,128)}, f32[3584,512]{1,0:T(8,128)}, f32[512,3584]{1,0:T(8,128)})) conditional(s32[]{:T(128)} %bitcast.45, (f32[3584,512]{1,0:T(8,128)}, f32[3584,512]{1,0:T(8,128)}, f32[512,3584]{1,0:T(8,128)}) %tuple.100, (s32[]{:T(128)}, bf16[1024,3584]{1,0:T(8,128)(2,1)}, bf16[1024,512]{1,0:T(8,128)(2,1)}, ...), branch_computations={%region_12.12_spmd, %region_13.13_spmd} | conditional | flops 1414791168 | bytes 105909384 | solution.py:114
  468.8 10.2 %convolution_add_fusion.2 = f32[3584,512]{1,0:T(8,128)} fusion(f32[3584,512]{1,0:T(8,128)} %get-tuple-element.538, bf16[1024,3584]{1,0:T(8,128)(2,1)} %get-tuple-element.535, s32[]{:T(128)S(6)} %select_n.35, bf16[1024,512]{1,0:T(8,128)(2,1)} %get-tuple-element.539), kind=kOutput, calls=%fused_computation.21 | convolution fusion | flops 471597056 | bytes 15729664 | tf_op jit(solution)/shard_map/while/body/eval_jaxpr/cond/branch_1_fun/dot_general | solution.py:33
  480.2 20.7 %conditional.5 = ((f32[3584,512]{1,0:T(8,128)}, f32[3584,512]{1,0:T(8,128)}, f32[512,3584]{1,0:T(8,128)})) conditional(s32[]{:T(128)} %bitcast.45, (f32[3584,512]{1,0:T(8,128)}, f32[3584,512]{1,0:T(8,128)}, f32[512,3584]{1,0:T(8,128)}) %tuple.100, (s32[]{:T(128)}, bf16[1024,3584]{1,0:T(8,128)(2,1)}, bf16[1024,512]{1,0:T(8,128)(2,1)}, ...), branch_computations={%region_12.12_spmd, %region_13.13_spmd} | conditional | flops 1414791168 | bytes 105909384 | solution.py:114
  490.7 10.2 %convolution_add_fusion.2 = f32[3584,512]{1,0:T(8,128)} fusion(f32[3584,512]{1,0:T(8,128)} %get-tuple-element.538, bf16[1024,3584]{1,0:T(8,128)(2,1)} %get-tuple-element.535, s32[]{:T(128)S(6)} %select_n.35, bf16[1024,512]{1,0:T(8,128)(2,1)} %get-tuple-element.539), kind=kOutput, calls=%fused_computation.21 | convolution fusion | flops 471597056 | bytes 15729664 | tf_op jit(solution)/shard_map/while/body/eval_jaxpr/cond/branch_1_fun/dot_general | solution.py:33
  502.2 20.7 %conditional.5 = ((f32[3584,512]{1,0:T(8,128)}, f32[3584,512]{1,0:T(8,128)}, f32[512,3584]{1,0:T(8,128)})) conditional(s32[]{:T(128)} %bitcast.45, (f32[3584,512]{1,0:T(8,128)}, f32[3584,512]{1,0:T(8,128)}, f32[512,3584]{1,0:T(8,128)}) %tuple.100, (s32[]{:T(128)}, bf16[1024,3584]{1,0:T(8,128)(2,1)}, bf16[1024,512]{1,0:T(8,128)(2,1)}, ...), branch_computations={%region_12.12_spmd, %region_13.13_spmd} | conditional | flops 1414791168 | bytes 105909384 | solution.py:114
  512.6 10.2 %convolution_add_fusion.2 = f32[3584,512]{1,0:T(8,128)} fusion(f32[3584,512]{1,0:T(8,128)} %get-tuple-element.538, bf16[1024,3584]{1,0:T(8,128)(2,1)} %get-tuple-element.535, s32[]{:T(128)S(6)} %select_n.35, bf16[1024,512]{1,0:T(8,128)(2,1)} %get-tuple-element.539), kind=kOutput, calls=%fused_computation.21 | convolution fusion | flops 471597056 | bytes 15729664 | tf_op jit(solution)/shard_map/while/body/eval_jaxpr/cond/branch_1_fun/dot_general | solution.py:33
  524.1 20.7 %conditional.5 = ((f32[3584,512]{1,0:T(8,128)}, f32[3584,512]{1,0:T(8,128)}, f32[512,3584]{1,0:T(8,128)})) conditional(s32[]{:T(128)} %bitcast.45, (f32[3584,512]{1,0:T(8,128)}, f32[3584,512]{1,0:T(8,128)}, f32[512,3584]{1,0:T(8,128)}) %tuple.100, (s32[]{:T(128)}, bf16[1024,3584]{1,0:T(8,128)(2,1)}, bf16[1024,512]{1,0:T(8,128)(2,1)}, ...), branch_computations={%region_12.12_spmd, %region_13.13_spmd} | conditional | flops 1414791168 | bytes 105909384 | solution.py:114
  534.6 10.2 %convolution_add_fusion.2 = f32[3584,512]{1,0:T(8,128)} fusion(f32[3584,512]{1,0:T(8,128)} %get-tuple-element.538, bf16[1024,3584]{1,0:T(8,128)(2,1)} %get-tuple-element.535, s32[]{:T(128)S(6)} %select_n.35, bf16[1024,512]{1,0:T(8,128)(2,1)} %get-tuple-element.539), kind=kOutput, calls=%fused_computation.21 | convolution fusion | flops 471597056 | bytes 15729664 | tf_op jit(solution)/shard_map/while/body/eval_jaxpr/cond/branch_1_fun/dot_general | solution.py:33
  546.0 20.7 %conditional.5 = ((f32[3584,512]{1,0:T(8,128)}, f32[3584,512]{1,0:T(8,128)}, f32[512,3584]{1,0:T(8,128)})) conditional(s32[]{:T(128)} %bitcast.45, (f32[3584,512]{1,0:T(8,128)}, f32[3584,512]{1,0:T(8,128)}, f32[512,3584]{1,0:T(8,128)}) %tuple.100, (s32[]{:T(128)}, bf16[1024,3584]{1,0:T(8,128)(2,1)}, bf16[1024,512]{1,0:T(8,128)(2,1)}, ...), branch_computations={%region_12.12_spmd, %region_13.13_spmd} | conditional | flops 1414791168 | bytes 105909384 | solution.py:114
  556.5 10.2 %convolution_add_fusion.2 = f32[3584,512]{1,0:T(8,128)} fusion(f32[3584,512]{1,0:T(8,128)} %get-tuple-element.538, bf16[1024,3584]{1,0:T(8,128)(2,1)} %get-tuple-element.535, s32[]{:T(128)S(6)} %select_n.35, bf16[1024,512]{1,0:T(8,128)(2,1)} %get-tuple-element.539), kind=kOutput, calls=%fused_computation.21 | convolution fusion | flops 471597056 | bytes 15729664 | tf_op jit(solution)/shard_map/while/body/eval_jaxpr/cond/branch_1_fun/dot_general | solution.py:33
  572.0 9.3 %convert_bitcast_fusion.1 = (bf16[1,3584,512]{2,1,0:T(8,128)(2,1)}, bf16[1,3584,512]{2,1,0:T(8,128)(2,1)}) fusion(f32[3584,512]{1,0:T(8,128)} %get-tuple-element.573, f32[3584,512]{1,0:T(8,128)} %get-tuple-element.572), kind=kLoop, calls=%fused_computation.36 | loop fusion | flops 3670016 | bytes 22020096 | tf_op jit(solution)/shard_map/broadcast_in_dim | solution.py:196
  (221 shorter events, 269.8 us)
Async XLA Ops:
  7.2 93.5 %copy-start = (bf16[256,3584]{1,0:T(8,128)(2,1)S(1)}, bf16[256,3584]{1,0:T(8,128)(2,1)}, u32[]{:S(2)}) copy-start(bf16[256,3584]{1,0:T(8,128)(2,1)} %param.15) | copy-start | bytes 5505028
  7.2 194.2 %all-gather.6.cloned.1.call-start = ((), (), s32[]{:S(2)}) async-start(), calls=%async_computation.6 | async-start | bytes 11010048 | tf_op jit(solution)/shard_map/all_gather | solution.py:162
  100.6 105.8 %all-gather.4.cloned.1.call-start = ((), (), s32[]{:S(2)}) async-start(), calls=%async_computation.5 | async-start | bytes 11010048 | tf_op jit(solution)/shard_map/all_gather | solution.py:161
  187.6 6.8 %copy-start.7 = (u32[32]{0:T(128)S(1)}, u32[32]{0:T(128)}, u32[]{:S(2)}) copy-start(u32[32]{0:T(128)} %constant.129) | copy-start | bytes 388
  188.3 10.1 %all-to-all-start = ((s32[16,1,1]{2,1,0:T(1,128)}), s32[16,1,1]{2,1,0:T(1,128)S(1)}, u32[]{:S(2)}, u32[]{:S(2)}) async-start(s32[16,1,1]{2,1,0:T(1,128)} %copy.17), calls=%async_computation | async-start | bytes 16384 | tf_op jit(solution)/shard_map/all_to_all | solution.py:158
  194.4 178.3 %reduce-scatter.2.cloned.1.call-start = ((), (), s32[]{:S(2)}) async-start(), calls=%async_computation.7 | async-start | bytes 11010048 | tf_op jit(solution)/shard_map/reduce_scatter | solution.py:177
  214.2 5.3 copy-start.6
  232.0 5.3 copy-start.6
  249.8 5.3 copy-start.6
  267.7 5.3 copy-start.6
  285.5 5.3 copy-start.6
  303.3 5.3 copy-start.6
  321.1 5.3 copy-start.6
  338.9 5.3 copy-start.6
  372.7 208.6 %all-to-all-start.3 = ((bf16[16,32,3584]{2,1,0:T(8,128)(2,1)}), bf16[16,32,3584]{2,1,0:T(8,128)(2,1)}, u32[]{:S(2)}, u32[]{:S(2)}) async-start(bf16[16,32,3584]{2,1,0:T(8,128)(2,1)} %reduce-scatter.2.cloned.1.call-done), calls=%async_computation.4 | async-start | bytes 7340032 | tf_op jit(solution)/shard_map/all_to_all | solution.py:183
  392.6 7.7 %copy-start.2 = (f32[512,3584]{1,0:T(8,128)S(1)}, f32[512,3584]{1,0:T(8,128)}, u32[]{:S(2)}) copy-start(f32[512,3584]{1,0:T(8,128)} %get-tuple-element.540) | copy-start | bytes 22020100 | tf_op jit(solution)/shard_map/while/body/eval_jaxpr/cond
  403.0 10.2 %copy-start.3 = (f32[512,3584]{1,0:T(8,128)}, f32[512,3584]{1,0:T(8,128)S(1)}, u32[]{:S(2)}) copy-start(f32[512,3584]{1,0:T(8,128)S(1)} %convolution_add_fusion.1) | copy-start | bytes 22020100 | tf_op jit(solution)/shard_map/while/body/eval_jaxpr/cond
  414.5 7.7 %copy-start.2 = (f32[512,3584]{1,0:T(8,128)S(1)}, f32[512,3584]{1,0:T(8,128)}, u32[]{:S(2)}) copy-start(f32[512,3584]{1,0:T(8,128)} %get-tuple-element.540) | copy-start | bytes 22020100 | tf_op jit(solution)/shard_map/while/body/eval_jaxpr/cond
  424.9 10.2 %copy-start.3 = (f32[512,3584]{1,0:T(8,128)}, f32[512,3584]{1,0:T(8,128)S(1)}, u32[]{:S(2)}) copy-start(f32[512,3584]{1,0:T(8,128)S(1)} %convolution_add_fusion.1) | copy-start | bytes 22020100 | tf_op jit(solution)/shard_map/while/body/eval_jaxpr/cond
  436.4 7.7 %copy-start.2 = (f32[512,3584]{1,0:T(8,128)S(1)}, f32[512,3584]{1,0:T(8,128)}, u32[]{:S(2)}) copy-start(f32[512,3584]{1,0:T(8,128)} %get-tuple-element.540) | copy-start | bytes 22020100 | tf_op jit(solution)/shard_map/while/body/eval_jaxpr/cond
  446.8 10.2 %copy-start.3 = (f32[512,3584]{1,0:T(8,128)}, f32[512,3584]{1,0:T(8,128)S(1)}, u32[]{:S(2)}) copy-start(f32[512,3584]{1,0:T(8,128)S(1)} %convolution_add_fusion.1) | copy-start | bytes 22020100 | tf_op jit(solution)/shard_map/while/body/eval_jaxpr/cond
  458.3 7.7 %copy-start.2 = (f32[512,3584]{1,0:T(8,128)S(1)}, f32[512,3584]{1,0:T(8,128)}, u32[]{:S(2)}) copy-start(f32[512,3584]{1,0:T(8,128)} %get-tuple-element.540) | copy-start | bytes 22020100 | tf_op jit(solution)/shard_map/while/body/eval_jaxpr/cond
  468.8 10.2 %copy-start.3 = (f32[512,3584]{1,0:T(8,128)}, f32[512,3584]{1,0:T(8,128)S(1)}, u32[]{:S(2)}) copy-start(f32[512,3584]{1,0:T(8,128)S(1)} %convolution_add_fusion.1) | copy-start | bytes 22020100 | tf_op jit(solution)/shard_map/while/body/eval_jaxpr/cond
  480.3 7.7 %copy-start.2 = (f32[512,3584]{1,0:T(8,128)S(1)}, f32[512,3584]{1,0:T(8,128)}, u32[]{:S(2)}) copy-start(f32[512,3584]{1,0:T(8,128)} %get-tuple-element.540) | copy-start | bytes 22020100 | tf_op jit(solution)/shard_map/while/body/eval_jaxpr/cond
  490.7 10.2 %copy-start.3 = (f32[512,3584]{1,0:T(8,128)}, f32[512,3584]{1,0:T(8,128)S(1)}, u32[]{:S(2)}) copy-start(f32[512,3584]{1,0:T(8,128)S(1)} %convolution_add_fusion.1) | copy-start | bytes 22020100 | tf_op jit(solution)/shard_map/while/body/eval_jaxpr/cond
  502.2 7.7 %copy-start.2 = (f32[512,3584]{1,0:T(8,128)S(1)}, f32[512,3584]{1,0:T(8,128)}, u32[]{:S(2)}) copy-start(f32[512,3584]{1,0:T(8,128)} %get-tuple-element.540) | copy-start | bytes 22020100 | tf_op jit(solution)/shard_map/while/body/eval_jaxpr/cond
  512.6 10.2 %copy-start.3 = (f32[512,3584]{1,0:T(8,128)}, f32[512,3584]{1,0:T(8,128)S(1)}, u32[]{:S(2)}) copy-start(f32[512,3584]{1,0:T(8,128)S(1)} %convolution_add_fusion.1) | copy-start | bytes 22020100 | tf_op jit(solution)/shard_map/while/body/eval_jaxpr/cond
  524.1 7.7 %copy-start.2 = (f32[512,3584]{1,0:T(8,128)S(1)}, f32[512,3584]{1,0:T(8,128)}, u32[]{:S(2)}) copy-start(f32[512,3584]{1,0:T(8,128)} %get-tuple-element.540) | copy-start | bytes 22020100 | tf_op jit(solution)/shard_map/while/body/eval_jaxpr/cond
  534.6 10.2 %copy-start.3 = (f32[512,3584]{1,0:T(8,128)}, f32[512,3584]{1,0:T(8,128)S(1)}, u32[]{:S(2)}) copy-start(f32[512,3584]{1,0:T(8,128)S(1)} %convolution_add_fusion.1) | copy-start | bytes 22020100 | tf_op jit(solution)/shard_map/while/body/eval_jaxpr/cond
  546.0 7.7 %copy-start.2 = (f32[512,3584]{1,0:T(8,128)S(1)}, f32[512,3584]{1,0:T(8,128)}, u32[]{:S(2)}) copy-start(f32[512,3584]{1,0:T(8,128)} %get-tuple-element.540) | copy-start | bytes 22020100 | tf_op jit(solution)/shard_map/while/body/eval_jaxpr/cond
  556.5 10.2 %copy-start.3 = (f32[512,3584]{1,0:T(8,128)}, f32[512,3584]{1,0:T(8,128)S(1)}, u32[]{:S(2)}) copy-start(f32[512,3584]{1,0:T(8,128)S(1)} %convolution_add_fusion.1) | copy-start | bytes 22020100 | tf_op jit(solution)/shard_map/while/body/eval_jaxpr/cond
  572.0 13.7 %copy-start.1 = (bf16[256,3584]{1,0:T(8,128)(2,1)S(1)}, bf16[256,3584]{1,0:T(8,128)(2,1)}, u32[]{:S(2)}) copy-start(bf16[256,3584]{1,0:T(8,128)(2,1)} %param.15) | copy-start | bytes 5505028
  (16 other events, 46.4 us)
Sparse Core Ops, SparseCore 0:
  100.7 18.5 all-gather.5
  187.8 18.5 all-gather.3
  355.6 17.0 reduce-scatter.1
where the time goes:
time: 595 us; the launch traced here: 592 us
  matrix products  276 us (46%)
  blocking collectives  175 us (29%)
  local copies, waits for them, and re-layouts  59 us (10%)
  waiting for transfers between devices  25 us (4%)
  other arithmetic  18.3 us (3%)
  between operations  14.5 us (2%)
  starting transfers between devices  13.1 us (2%)
  loops' own time  11.4 us (2%)
    all_to_all x1, blocking collectives, local(): lax.all_to_all(sent_cots, 'expert', split_axis=0, concat_axis=0, tiled=True)  87.5 us
    all_to_all x1, blocking collectives, local(): lax.all_to_all(sent_rows, 'expert', split_axis=0, concat_axis=0, tiled=True)  85.8 us
    dot_general x8, matrix products, weight_sums(): lax.dot_general(rows_x, d_up, (((0,), (0,)), ((), ())), preferred_element...  81.5 us
    dot_general x8, matrix products, weight_sums(): lax.dot_general(rows_x, d_gate, (((0,), (0,)), ((), ())), preferred_eleme...  61.1 us
    dynamic_update_slice x24, local copies, waits for them, and re-layouts, add_tile(): lax.dynamic_update_slice_in_dim(whole, piece, start, 0)  26.8 us
    dot_general x8, matrix products, front_rows(): lax.dot_general(rows_cot, down_w, (((1,), (1,)), ((), ())), preferred_ele...  25.7 us
    dot_general x8, matrix products, front_rows(): up_pre = jnp.dot(rows_x, up_w, preferred_element_type=jnp.float32)  24.9 us
    dot_general x8, matrix products, weight_sums(): lax.dot_general(hidden, rows_cot, (((0,), (0,)), ((), ())), preferred_ele...  22.2 us
  transfers between devices with their start and end apart: 5, of which 3 were waited for; matrix products, arithmetic and copies ran while one was open for 34% of the time, Pallas kernels for 0%

commit v1 on v0

v1 whole, which is shorter than its diff:
```python
import jax
import jax.numpy as jnp
from jax import lax
from jax.sharding import PartitionSpec as P


def front_rows(rows_x, rows_cot, gate_w, up_w, down_w):
    gate_pre = jnp.dot(rows_x, gate_w, preferred_element_type=jnp.float32)
    up_pre = jnp.dot(rows_x, up_w, preferred_element_type=jnp.float32)
    sigmoid_gate = jax.nn.sigmoid(gate_pre)
    swish_gate = gate_pre * sigmoid_gate
    hidden = (swish_gate * up_pre).astype(jnp.bfloat16)
    d_hidden = lax.dot_general(
        rows_cot, down_w, (((1,), (1,)), ((), ())), preferred_element_type=jnp.float32
    )
    d_gate = (d_hidden * up_pre * sigmoid_gate * (1.0 + gate_pre * (1.0 - sigmoid_gate))).astype(
        jnp.bfloat16
    )
    d_up = (d_hidden * swish_gate).astype(jnp.bfloat16)
    dx_part = lax.dot_general(
        d_gate, gate_w, (((1,), (1,)), ((), ())), preferred_element_type=jnp.float32
    )
    dx_part = dx_part + lax.dot_general(
        d_up, up_w, (((1,), (1,)), ((), ())), preferred_element_type=jnp.float32
    )
    return (hidden, d_gate, d_up, dx_part.astype(jnp.bfloat16))


def weight_sums(rows_x, rows_cot, hidden, d_gate, d_up):
    grad_gate = lax.dot_general(
        rows_x, d_gate, (((0,), (0,)), ((), ())), preferred_element_type=jnp.float32
    )
    grad_up = lax.dot_general(
        rows_x, d_up, (((0,), (0,)), ((), ())), preferred_element_type=jnp.float32
    )
    grad_down = lax.dot_general(
        hidden, rows_cot, (((0,), (0,)), ((), ())), preferred_element_type=jnp.float32
    )
    return (grad_gate, grad_up, grad_down)


def local(tokens, cotangent, expert_ids, gate_probs, w_gate, w_up, w_down):
    owners = lax.axis_size("expert")
    groups = lax.axis_size("dp")
    tok_rows = tokens.shape[0]
    model_width = tokens.shape[1]
    fanout = expert_ids.shape[1]
    capacity = max(2, 2 * tok_rows * fanout // owners)
    copies = tok_rows * fanout
    flat_ids = expert_ids.reshape(copies)
    onehot = (flat_ids[:, None] == jnp.arange(owners, dtype=jnp.int32)[None, :]).astype(jnp.int32)
    before = jnp.cumsum(onehot, axis=0) - onehot
    slot_rank = jnp.sum(before * onehot, axis=1)
    position = flat_ids * capacity + slot_rank
    copy_rows = tokens[:, None, :].reshape(copies, model_width)
    copy_tok_cot = cotangent[:, None, :].reshape(copies, model_width)
    copy_cots = (gate_probs * copy_tok_cot.astype(jnp.float32)).astype(jnp.bfloat16)
    placing = (jnp.arange(owners * capacity, dtype=jnp.int32)[:, None] == position[None, :]).astype(
        jnp.bfloat16
    )
    sent_rows = (
        jnp.dot(placing, copy_rows, preferred_element_type=jnp.float32)
        .astype(jnp.bfloat16)
        .reshape(owners, capacity, model_width)
    )
    sent_cots = (
        jnp.dot(placing, copy_cots, preferred_element_type=jnp.float32)
        .astype(jnp.bfloat16)
        .reshape(owners, capacity, model_width)
    )
    came_rows = lax.all_to_all(sent_rows, "expert", split_axis=0, concat_axis=0, tiled=True)
    came_cots = lax.all_to_all(sent_cots, "expert", split_axis=0, concat_axis=0, tiled=True)
    got_rows = lax.all_gather(came_rows, "dp", axis=0, tiled=True)
    got_cots = lax.all_gather(came_cots, "dp", axis=0, tiled=True)
    slots_all = owners * groups * capacity
    rows_x = got_rows.reshape(slots_all, model_width)
    rows_cot = got_cots.reshape(slots_all, model_width)
    hidden, d_gate, d_up, dx_part = front_rows(rows_x, rows_cot, w_gate[0], w_up[0], w_down[0])
    summed = lax.psum_scatter(
        dx_part.reshape(groups * owners, capacity, model_width),
        "dp",
        scatter_dimension=0,
        tiled=True,
    )
    returned = lax.all_to_all(summed, "expert", split_axis=0, concat_axis=0, tiled=True)
    grad_gate, grad_up, grad_down = weight_sums(rows_x, rows_cot, hidden, d_gate, d_up)
    copy_grad = lax.dot_general(
        placing,
        returned.reshape(owners * capacity, model_width),
        (((0,), (0,)), ((), ())),
        preferred_element_type=jnp.float32,
    )
    grad_tokens = jnp.sum(copy_grad.reshape(tok_rows, fanout, model_width), axis=1).astype(
        jnp.bfloat16
    )
    return (
        grad_tokens,
        grad_gate.astype(jnp.bfloat16)[None],
        grad_up.astype(jnp.bfloat16)[None],
        grad_down.astype(jnp.bfloat16)[None],
    )


def solution(mesh):
    return jax.shard_map(
        local,
        mesh=mesh,
        in_specs=(
            P(("dp", "expert"), None),
            P(("dp", "expert"), None),
            P(("dp", "expert"), None),
            P(("dp", "expert"), None),
            P("expert", None, "dp"),
            P("expert", None, "dp"),
            P("expert", "dp", None),
        ),
        out_specs=(
            P(("dp", "expert"), None),
            P("expert", None, "dp"),
            P("expert", None, "dp"),
            P("expert", "dp", None),
        ),
        check_vma=False,
    )
```

time: 595 us -> 353 us (0.59)
  matrix products: 276 us -> 71.7 us
  local copies, waits for them, and re-layouts: 59 us -> 1.67 us
  waiting for transfers between devices: 25 us -> 81.8 us
  other arithmetic: 18.3 us -> 2.87 us
  loops' own time: 11.4 us -> 0 us
    dot_general x8 -> x1, matrix products: 81.5 us -> 8.77 us  [weight_sums(): lax.dot_general(rows_x, d_up, (((0,), (0,)), ((), ())), preferred_element...]
    all_to_all x1, waiting for transfers between devices: 0.01 us -> 61 us  [local(): lax.all_to_all(summed, 'expert', split_axis=0, concat_axis=0, tiled=True)]
    dot_general x8 -> x1, matrix products: 61.1 us -> 8.76 us  [weight_sums(): lax.dot_general(rows_x, d_gate, (((0,), (0,)), ((), ())), preferred_eleme...]
    dynamic_update_slice x24 -> x0, local copies, waits for them, and re-layouts: 26.8 us -> none  [add_tile(): lax.dynamic_update_slice_in_dim(whole, piece, start, 0)]
    dot_general x8 -> x1, matrix products: 24.9 us -> 5.29 us  [front_rows(): up_pre = jnp.dot(rows_x, up_w, preferred_element_type=jnp.float32)]
    dot_general x8 -> x1, matrix products: 22.2 us -> 5.84 us  [weight_sums(): lax.dot_general(hidden, rows_cot, (((0,), (0,)), ((), ())), preferred_ele...]
    dot_general x8 -> x1, matrix products: 25.7 us -> 10.1 us  [front_rows(): lax.dot_general(rows_cot, down_w, (((1,), (1,)), ((), ())), preferred_ele...]
    broadcast_in_dim x2 -> x0, other arithmetic: 14.6 us -> none  [the longest x1 9.29 us: local(): grad_up.astype(jnp.bfloat16)[None]]
  transfers between devices with their start and end apart: 5 -> 4, of which waited for: 3 -> 3; matrix products, arithmetic and copies ran while one was open for 34% -> 11% of each run, Pallas kernels for 0% -> 0%
where the time goes in v1:
time: 353 us; the launch traced here: 352 us
  blocking collectives  173 us (49%)
  waiting for transfers between devices  81.8 us (23%)
  matrix products  71.7 us (20%)
  between operations  13.9 us (4%)
  starting transfers between devices  7.26 us (2%)
    all_to_all x1, blocking collectives, local(): lax.all_to_all(sent_rows, 'expert', split_axis=0, concat_axis=0, tiled=True)  87.5 us
    all_to_all x1, blocking collectives, local(): lax.all_to_all(sent_cots, 'expert', split_axis=0, concat_axis=0, tiled=True)  85.8 us
    all_to_all x1, waiting for transfers between devices, local(): lax.all_to_all(summed, 'expert', split_axis=0, concat_axis=0, tiled=True)  61 us
    reduce_scatter x1, waiting for transfers between devices, local(): lax.psum_scatter(dx_part.reshape(groups * owners, capacity, model_width),...  17.2 us
    dot_general x1, matrix products, front_rows(): lax.dot_general(rows_cot, down_w, (((1,), (1,)), ((), ())), preferred_ele...  10.1 us
    dot_general x1, matrix products, front_rows(): gate_pre = jnp.dot(rows_x, gate_w, preferred_element_type=jnp.float32)  9.53 us
    dot_general x1, matrix products, front_rows(): lax.dot_general(d_up, up_w, (((1,), (1,)), ((), ())), preferred_element_t...  9.26 us
    dot_general x1, matrix products, weight_sums(): lax.dot_general(rows_x, d_up, (((0,), (0,)), ((), ())), preferred_element...  8.77 us
  transfers between devices with their start and end apart: 4, of which 3 were waited for; matrix products, arithmetic and copies ran while one was open for 11% of the time, Pallas kernels for 0%

profile of v1, /device:TPU:14, one launch (start us, length us, event | category | flops | bytes accessed | tf_op | source)
XLA Modules:
  0.0 352.4 jit_solution(1378786222437827949)
XLA Ops:
  7.2 0.0 copy-start
  7.2 0.0 all-gather.5.cloned.1.call-start
  7.2 0.8 fusion.21
  8.0 0.6 reduce-window.6
  8.6 0.2 slice_reduce_fusion
  8.8 0.8 fusion.20
  9.6 0.7 multiply_add_fusion
  10.3 1.1 convolution_convert_fusion
  11.4 87.5 %all_to_all.15 = bf16[16,32,3584]{2,1,0:T(8,128)(2,1)} all-to-all(bf16[16,32,3584]{2,1,0:T(8,128)(2,1)S(1)} %bitcast.62), channel_id=1, replica_groups=mesh['dp'=2,'expert'=16] {'expert'}, dimensions={0} | all-to-all | bytes 7340032 | tf_op jit(solution)/shard_map/all_to_all | solution.py:71
  98.9 0.0 all-gather.5.cloned.1.call-update
  98.9 0.0 all-gather.3.cloned.1.call-start
  99.0 1.4 copy-done.2
  100.4 1.2 convolution_convert_fusion.1
  101.6 85.8 %all_to_all.16 = bf16[16,32,3584]{2,1,0:T(8,128)(2,1)} all-to-all(bf16[16,32,3584]{2,1,0:T(8,128)(2,1)S(1)} %bitcast.61), channel_id=1, replica_groups=mesh['dp'=2,'expert'=16] {'expert'}, dimensions={0} | all-to-all | bytes 7340032 | tf_op jit(solution)/shard_map/all_to_all | solution.py:72
  187.4 0.0 all-gather.3.cloned.1.call-update
  187.5 0.2 reduce-scatter.2.cloned.1.call-start
  187.7 0.0 all-gather.5.cloned.1.call-done
  187.7 0.0 copy-start.6
  187.7 9.5 %fusion.5 = f32[1024,512]{1,0:T(8,128)} fusion(bf16[1024,3584]{1,0:T(8,128)(2,1)} %bitcast.68, bf16[1,3584,512]{2,1,0:T(8,128)(2,1)} %param.11), kind=kOutput, calls=%fused_computation.12 | convolution fusion | flops 3758096384 | bytes 13107200 | tf_op jit(solution)/shard_map/dot_general | solution.py:8
  197.3 5.3 %fusion.8 = f32[1024,512]{1,0:T(8,128)} fusion(bf16[1024,3584]{1,0:T(8,128)(2,1)S(1)} %bitcast.71, bf16[1,3584,512]{2,1,0:T(8,128)(2,1)S(1)} %copy-done.6), kind=kOutput, calls=%fused_computation.15 | convolution fusion | flops 3758096384 | bytes 13107200 | tf_op jit(solution)/shard_map/dot_general | solution.py:9
  202.6 3.6 %all-gather.3.cloned.1.call-done = bf16[32,32,3584]{2,1,0:T(8,128)(2,1)} async-done(((bf16[16,32,3584]{2,1,0:T(8,128)(2,1)}), bf16[32,32,3584]{2,1,0:T(8,128)(2,1)}) %all-gather.3.cloned.1.call-update) | async-done | bytes 7340048 | tf_op jit(solution)/shard_map/all_gather | solution.py:74
  206.2 10.1 %multiply_convert_fusion.2 = (bf16[1024,512]{1,0:T(8,128)(2,1)S(1)}, bf16[1024,512]{1,0:T(8,128)(2,1)S(1)}) fusion(f32[1024,512]{1,0:T(8,128)} %fusion.5, f32[1024,512]{1,0:T(8,128)} %fusion.8, bf16[1024,3584]{1,0:T(8,128)(2,1)} %bitcast.72, bf16[1,512,3584]{2,1,0:T(8,128)(2,1)} %param.13), kind=kOutput, calls=%fused_computation.21 | convolution fusion | flops 3764912128 | bytes 17301504 | tf_op jit(solution)/shard_map/dot_general | solution.py:13
  216.4 7.4 %fusion.3 = f32[1024,3584]{1,0:T(8,128)} fusion(bf16[1024,512]{1,0:T(8,128)(2,1)S(1)} %get-tuple-element.5, bf16[1,3584,512]{2,1,0:T(8,128)(2,1)S(1)} %copy-done.5), kind=kOutput, calls=%fused_computation.10 | convolution fusion | flops 3758096384 | bytes 19398656 | tf_op jit(solution)/shard_map/dot_general | solution.py:20
  223.7 9.3 %add_convert_fusion = bf16[1024,3584]{1,0:T(8,128)(2,1)} fusion(f32[1024,3584]{1,0:T(8,128)} %fusion.3, bf16[1024,512]{1,0:T(8,128)(2,1)S(1)} %get-tuple-element.4, bf16[1,3584,512]{2,1,0:T(8,128)(2,1)S(1)} %copy-done.7), kind=kOutput, calls=%fused_computation | convolution fusion | flops 3765436416 | bytes 26738688 | tf_op jit(solution)/shard_map/dot_general | solution.py:23
  233.0 0.0 reduce-scatter.2.cloned.1.call-update
  233.0 17.2 %reduce-scatter.2.cloned.1.call-done = bf16[16,32,3584]{2,1,0:T(8,128)(2,1)} async-done(((bf16[32,32,3584]{2,1,0:T(8,128)(2,1)}), bf16[16,32,3584]{2,1,0:T(8,128)(2,1)}) %reduce-scatter.2.cloned.1.call-update) | async-done | bytes 3670032 | tf_op jit(solution)/shard_map/reduce_scatter | solution.py:79
  250.1 7.0 %all-to-all-start.2 = ((bf16[16,32,3584]{2,1,0:T(8,128)(2,1)}), bf16[16,32,3584]{2,1,0:T(8,128)(2,1)}, u32[]{:S(2)}, u32[]{:S(2)}) async-start(bf16[16,32,3584]{2,1,0:T(8,128)(2,1)} %reduce-scatter.2.cloned.1.call-done), calls=%async_computation.3 | async-start | bytes 7340032 | tf_op jit(solution)/shard_map/all_to_all | solution.py:85
  257.1 8.8 %fusion.1 = bf16[1,3584,512]{2,1,0:T(8,128)(2,1)} fusion(bf16[1024,3584]{1,0:T(8,128)(2,1)} %bitcast.69, bf16[1024,512]{1,0:T(8,128)(2,1)S(1)} %get-tuple-element.4), kind=kOutput, calls=%fused_computation.7 | convolution fusion | flops 3759931392 | bytes 12058624 | tf_op jit(solution)/shard_map/dot_general | solution.py:33
  265.9 8.8 %fusion = bf16[1,3584,512]{2,1,0:T(8,128)(2,1)} fusion(bf16[1024,3584]{1,0:T(8,128)(2,1)} %bitcast.70, bf16[1024,512]{1,0:T(8,128)(2,1)S(1)} %get-tuple-element.5), kind=kOutput, calls=%fused_computation.6 | convolution fusion | flops 3759931392 | bytes 12058624 | tf_op jit(solution)/shard_map/dot_general | solution.py:30
  274.7 5.8 %fusion.2 = bf16[1,512,3584]{2,1,0:T(8,128)(2,1)} fusion(bf16[1024,3584]{1,0:T(8,128)(2,1)S(1)} %bitcast.75, f32[1024,512]{1,0:T(8,128)S(1)} %copy-done.9, f32[1024,512]{1,0:T(8,128)S(1)} %copy-done.8), kind=kOutput, calls=%fused_computation.8 | convolution fusion | flops 3763077120 | bytes 15204352 | tf_op jit(solution)/shard_map/dot_general | solution.py:36
  280.5 61.0 %all-to-all-done.2 = bf16[16,32,3584]{2,1,0:T(8,128)(2,1)} async-done(((bf16[16,32,3584]{2,1,0:T(8,128)(2,1)}), bf16[16,32,3584]{2,1,0:T(8,128)(2,1)}, u32[]{:S(2)}, u32[]{:S(2)}) %all-to-all-start.2) | async-done | bytes 3670048 | tf_op jit(solution)/shard_map/all_to_all | solution.py:85
  341.5 4.4 %convolution_convert_fusion.5 = bf16[256,3584]{1,0:T(8,128)(2,1)} fusion(bf16[512,3584]{1,0:T(8,128)(2,1)} %bitcast.12, s32[256]{0:T(256)S(1)} %multiply_add_fusion), kind=kOutput, calls=%fused_computation.9 | convolution fusion | flops 940572672 | bytes 5506048 | tf_op jit(solution)/shard_map/dot_general | solution.py:87
  (24 shorter events, 0.1 us)
Async XLA Ops:
  7.2 3.1 copy-start
  7.2 180.5 %all-gather.5.cloned.1.call-start = ((), (), s32[]{:S(2)}) async-start(), calls=%async_computation.5 | async-start | bytes 11010048 | tf_op jit(solution)/shard_map/all_gather | solution.py:73
  98.9 1.5 copy-start.2
  98.9 1.5 copy-start.3
  98.9 107.3 %all-gather.3.cloned.1.call-start = ((), (), s32[]{:S(2)}) async-start(), calls=%async_computation.4 | async-start | bytes 11010048 | tf_op jit(solution)/shard_map/all_gather | solution.py:74
  187.5 62.7 %reduce-scatter.2.cloned.1.call-start = ((), (), s32[]{:S(2)}) async-start(), calls=%async_computation.6 | async-start | bytes 11010048 | tf_op jit(solution)/shard_map/reduce_scatter | solution.py:79
  187.7 9.6 %copy-start.4 = (bf16[32,32,3584]{2,1,0:T(8,128)(2,1)S(1)}, bf16[32,32,3584]{2,1,0:T(8,128)(2,1)}, u32[]{:S(2)}) copy-start(bf16[32,32,3584]{2,1,0:T(8,128)(2,1)} %all-gather.5.cloned.1.call-done) | copy-start | bytes 22020100
  187.7 9.5 %copy-start.6 = (bf16[1,3584,512]{2,1,0:T(8,128)(2,1)S(1)}, bf16[1,3584,512]{2,1,0:T(8,128)(2,1)}, u32[]{:S(2)}) copy-start(bf16[1,3584,512]{2,1,0:T(8,128)(2,1)} %param.12) | copy-start | bytes 11010052
  206.2 10.1 %copy-start.5 = (bf16[1,3584,512]{2,1,0:T(8,128)(2,1)S(1)}, bf16[1,3584,512]{2,1,0:T(8,128)(2,1)}, u32[]{:S(2)}) copy-start(bf16[1,3584,512]{2,1,0:T(8,128)(2,1)} %param.11) | copy-start | bytes 11010052
  216.3 7.4 %copy-start.7 = (bf16[1,3584,512]{2,1,0:T(8,128)(2,1)S(1)}, bf16[1,3584,512]{2,1,0:T(8,128)(2,1)}, u32[]{:S(2)}) copy-start(bf16[1,3584,512]{2,1,0:T(8,128)(2,1)} %param.12) | copy-start | bytes 11010052
  250.1 91.3 %all-to-all-start.2 = ((bf16[16,32,3584]{2,1,0:T(8,128)(2,1)}), bf16[16,32,3584]{2,1,0:T(8,128)(2,1)}, u32[]{:S(2)}, u32[]{:S(2)}) async-start(bf16[16,32,3584]{2,1,0:T(8,128)(2,1)} %reduce-scatter.2.cloned.1.call-done), calls=%async_computation.3 | async-start | bytes 7340032 | tf_op jit(solution)/shard_map/all_to_all | solution.py:85
  257.1 17.5 %slice-start = ((s8[7340032]{0:T(1024)(128)(4,1)}), s8[4194304]{0:T(1024)(128)(4,1)S(1)}, s32[]{:S(2)}) async-start(s8[7340032]{0:T(1024)(128)(4,1)} %bitcast.73), calls=%async_computation.7 | async-start | bytes 8388608
  265.9 8.8 %slice-start.1 = ((s8[7340032]{0:T(1024)(128)(4,1)}), s8[3145728]{0:T(1024)(128)(4,1)S(1)}, s32[]{:S(2)}) async-start(s8[7340032]{0:T(1024)(128)(4,1)} %bitcast.73), calls=%async_computation.8 | async-start | bytes 6291456
  265.9 8.8 %copy-start.8 = (f32[1024,512]{1,0:T(8,128)S(1)}, f32[1024,512]{1,0:T(8,128)}, u32[]{:S(2)}) copy-start(f32[1024,512]{1,0:T(8,128)} %fusion.5) | copy-start | bytes 6291460
  265.9 8.8 %copy-start.9 = (f32[1024,512]{1,0:T(8,128)S(1)}, f32[1024,512]{1,0:T(8,128)}, u32[]{:S(2)}) copy-start(f32[1024,512]{1,0:T(8,128)} %fusion.8) | copy-start | bytes 6291460
  274.7 71.2 %copy-start.1 = (bf16[256,3584]{1,0:T(8,128)(2,1)S(1)}, bf16[256,3584]{1,0:T(8,128)(2,1)}, u32[]{:S(2)}) copy-start(bf16[256,3584]{1,0:T(8,128)(2,1)} %param.7) | copy-start | bytes 5505028
Sparse Core Ops, SparseCore 0:
  99.0 18.5 all-gather.4
  187.6 18.5 all-gather.2
  233.1 16.9 reduce-scatter.1
